TPU v7x, 32 devices: a whole 2x2x4 slice. The times are simulated.
32 devices in a mesh: dp: 8 (over z, x), tensor: 4 (over y, core).
Axes of the slice: x: 2, y: 2, z: 4, core: 2. Of those that a mesh axis runs over, the one named last changes fastest.
Arguments:
- tokens: bfloat16 [8192, 1024], P(('dp', 'tensor')), may hold values from -6 to 6
- segments: int32 [8, 1024], P('dp'), may hold values from 0 to 3, never falling along the last dimension, each value on 1 to 512 neighbouring positions
- cotangent: bfloat16 [8192, 1024], P(('dp', 'tensor')), may hold values from -6 to 6
- timestep_norm_gain: float32 [1024], replicated, may hold values from 0.5 to 1.5
- ema_alpha: float32 [1024, 16], P('tensor'), may hold values from 0.05 to 0.95
- ema_delta: float32 [1024, 16], P('tensor'), may hold values from 0.05 to 0.95
- ema_theta: float32 [1024, 16], P('tensor'), may hold values from -1 to 1
- ema_beta: float32 [1024, 16], P('tensor'), may hold values from -3 to 3
- eta_real: float32 [1024, 16], P('tensor'), may hold values from -1 to 1
- eta_imag: float32 [1024, 16], P('tensor'), may hold values from -1 to 1
- ema_omega: float32 [1024], P('tensor'), may hold values from -2 to 2
- w_shared: bfloat16 [1024, 256], P('tensor'), may hold values from -0.1875 to 0.1875
- q_gain: float32 [256], replicated, may hold values from 0.5 to 1.5
- q_bias: float32 [256], replicated, may hold values from -2 to 2
- k_gain: float32 [256], replicated, may hold values from 0.5 to 1.5
- w_attgate: bfloat16 [1024, 2048], P(None, 'tensor'), may hold values from -0.1875 to 0.1875
- w_value: bfloat16 [1024, 2048], P(None, 'tensor'), may hold values from -0.1875 to 0.1875
- w_attout: bfloat16 [2048, 1024], P('tensor'), may hold values from -0.75 to 0.75
- rms_gain: float32 [1024], replicated, may hold values from 0.5 to 1.5
- w_gate: bfloat16 [1024, 2560], P(None, 'tensor'), may hold values from -0.1875 to 0.1875
- w_up: bfloat16 [1024, 2560], P(None, 'tensor'), may hold values from -0.1875 to 0.1875
- w_down: bfloat16 [2560, 1024], P('tensor'), may hold values from -0.25 to 0.25
Outputs:
- output: bfloat16 [8192, 1024], P(('dp', 'tensor'))
- grad_tokens: bfloat16 [8192, 1024], P(('dp', 'tensor'))
- grad_norm_gain: float32 [1024], replicated
- grad_alpha: float32 [1024, 16], P('tensor')
- grad_delta: float32 [1024, 16], P('tensor')
- grad_theta: float32 [1024, 16], P('tensor')
- grad_beta: float32 [1024, 16], P('tensor')
- grad_eta_real: float32 [1024, 16], P('tensor')
- grad_eta_imag: float32 [1024, 16], P('tensor')
- grad_omega: float32 [1024], P('tensor')
- grad_shared: float32 [1024, 256], P('tensor')
- grad_q_gain: float32 [256], replicated
- grad_q_bias: float32 [256], replicated
- grad_k_gain: float32 [256], replicated
- grad_attgate: float32 [1024, 2048], P(None, 'tensor')
- grad_value: float32 [1024, 2048], P(None, 'tensor')
- grad_attout: float32 [2048, 1024], P('tensor')
- grad_rms_gain: float32 [1024], replicated
- grad_gate: float32 [1024, 2560], P(None, 'tensor')
- grad_up: float32 [1024, 2560], P(None, 'tensor')
- grad_down: float32 [2560, 1024], P('tensor')
Inputs may be any that keep to these rules, and one draw needn't show every extreme that they name: `segments`: within each row segment numbers never fall; each of the 4 documents has 1 to 512 tokens and one has exactly 512.
All inputs are finite; a program needn't handle non-finite values.
Results may differ from a plain program's by a relative error of at most 0.017.
Values may be sent and summed in bfloat16 or wider, within the bound.
A program may use at most 256 MiB of HBM per device.

v0:
```python
import functools
import math
import types

import jax
import jax.numpy as jnp
from jax import lax
from jax.experimental import pallas as pl
from jax.experimental.pallas import tpu as pltpu
from jax.sharding import PartitionSpec as P

epsilon = 1e-05
masked_score = -1000000000.0
f32 = jnp.float32
bf16 = jnp.bfloat16
MESH = pl.DeviceIdType.MESH
LANES = 128
SUB = 8
SPAN = 64
MAX_DOC = 512
PACK_TAIL = 32
VMEM_BYTES = 62 * 2**20


def plain(left, right):
    return jnp.dot(left, right, preferred_element_type=f32)


def cross(left, right):
    return lax.dot_general(
        left, right, (((1,), (1,)), ((), ())), preferred_element_type=f32
    )


def inner(left, right):
    return lax.dot_general(
        left, right, (((0,), (0,)), ((), ())), preferred_element_type=f32
    )


def sigmoid(value):
    return 1.0 / (1.0 + jnp.exp(-value))


def at(index, size):
    return pl.ds(pl.multiple_of(index * size, size), size)


class Stage:
    def __init__(self, ins, outs, bare, scratch, alias, refs):
        self.pending = {}
        self.flushed = []
        count = len(ins)
        self.hbm_in = dict(zip(ins, refs[:count]))
        total = len(outs) + len(bare)
        self.hbm_out = dict(zip(list(outs) + list(bare), refs[count : count + total]))
        rest = refs[count + total :]
        names = list(ins) + list(outs) + list(scratch)
        self.refs = dict(zip(names, rest[: len(names)]))
        self.load_sem, self.flush_sem, self.send_sem, self.recv_sem = rest[len(names) :]
        self.order = {name: k for k, name in enumerate(ins)}
        self.out_order = {name: k for k, name in enumerate(self.hbm_out)}
        self.sends = self.receipts = 0
        self.sets = {}
        self.names = {id(ref): name for name, ref in self.refs.items()}
        for name, other in alias:
            self.refs[name] = self.refs[other]

    def __getitem__(self, name):
        return self.refs[name]

    def __getattr__(self, name):
        return self.refs[name]

    def load(self, *refs):
        for name in [self.names[id(ref)] for ref in refs]:
            copy = pltpu.make_async_copy(
                self.hbm_in[name], self.refs[name], self.load_sem.at[self.order[name]]
            )
            copy.start()
            self.pending[name] = copy

    def need(self, *refs):
        for name in [self.names[id(ref)] for ref in refs]:
            copy = self.pending.pop(name, None)
            if copy is not None:
                copy.wait()

    def flush(self, *refs):
        for name in [self.names[id(ref)] for ref in refs]:
            if name in self.hbm_out:
                self.store(self.refs[name], name)

    def store(self, source, name):
        copy = pltpu.make_async_copy(
            source, self.hbm_out[name], self.flush_sem.at[self.out_order[name]]
        )
        copy.start()
        self.flushed.append(copy)

    def close(self):
        assert self.sends <= self.send_sem.shape[0]
        assert self.receipts <= self.recv_sem.shape[0]
        for copy in self.flushed:
            copy.wait()


    def sems(self, count, sends=None, key=None):
        if key in self.sets:
            return self.sets[key]
        first = self.sends, self.receipts
        self.sends += count if sends is None else sends
        self.receipts += count
        if key:
            self.sets[key] = first
        return first

    def remote(self, source, target_ref, base, index, device, sent=None):
        return pltpu.make_async_remote_copy(
            src_ref=source,
            dst_ref=target_ref,
            send_sem=self.send_sem.at[base[0] + (index if sent is None else sent)],
            recv_sem=self.recv_sem.at[base[1] + index],
            device_id=device,
            device_id_type=MESH,
        )


def run_stage(body, ins, outs, scratch, sems, collective, bare=(), alias=()):
    ins = vars(ins)
    written = {**outs, **dict(bare)}

    def kernel(*refs):
        body(Stage(list(ins), list(outs), list(dict(bare)), list(scratch), alias, refs))

    buffers = [pltpu.VMEM(array.shape, array.dtype) for array in ins.values()]
    buffers += [pltpu.VMEM(shape, kind) for shape, kind in outs.values()]
    buffers += [pltpu.VMEM(shape, kind) for shape, kind in scratch.values()]
    results = pl.pallas_call(
        kernel,
        out_shape=tuple(jax.ShapeDtypeStruct(shape, kind) for shape, kind in written.values()),
        in_specs=[pl.BlockSpec(memory_space=pl.ANY)] * len(ins),
        out_specs=tuple(pl.BlockSpec(memory_space=pl.ANY) for _ in written),
        scratch_shapes=buffers
        + [
            pltpu.SemaphoreType.DMA((len(ins),)),
            pltpu.SemaphoreType.DMA((len(written),)),
            pltpu.SemaphoreType.DMA((max(sems[0], 1),)),
            pltpu.SemaphoreType.DMA((max(sems[1], 1),)),
        ],
        compiler_params=pltpu.CompilerParams(
            collective_id=collective,
            has_side_effects=collective is not None,
            vmem_limit_bytes=VMEM_BYTES,
        ),
    )(*ins.values())
    return types.SimpleNamespace(**dict(zip(written, results)))


class Group:
    def __init__(self):
        self.me = lax.axis_index("tensor")
        chip = self.me // 2
        core = self.me % 2
        self.sib = chip * 2 + (1 - core)
        self.opp = (1 - chip) * 2 + core
        self.diag = (1 - chip) * 2 + (1 - core)

    def greet(self, more=()):
        barrier = pltpu.get_barrier_semaphore()
        for device in more:
            pl.semaphore_signal(barrier, inc=1, device_id={"dp": device}, device_id_type=MESH)
        for device in (self.sib, self.opp, self.diag):
            pl.semaphore_signal(barrier, inc=1, device_id={"tensor": device}, device_id_type=MESH)
        pl.semaphore_wait(barrier, 3 + len(more))


class Gather:
    def __init__(self, stage, group, source, place, pieces, key=None):
        self.g = group
        self.pieces = pieces
        base = stage.sems(3 * pieces, key=key)
        opp = {"tensor": group.opp}
        sib = {"tensor": group.sib}
        self.to_opp = [
            stage.remote(source(s), place(group.me, s), base, s, opp) for s in range(pieces)
        ]
        self.to_sib = [
            stage.remote(source(s), place(group.me, s), base, pieces + s, sib)
            for s in range(pieces)
        ]
        self.passed = [
            stage.remote(place(group.opp, s), place(group.opp, s), base, 2 * pieces + s, sib)
            for s in range(pieces)
        ]

    def send(self, s):
        self.to_opp[s].start()
        self.to_sib[s].start()

    def forward(self, s):
        self.to_opp[s].wait_recv()
        self.passed[s].start()

    def near(self):
        for s in range(self.pieces):
            self.to_sib[s].wait_recv()

    def far(self):
        for s in range(self.pieces):
            self.passed[s].wait_recv()

    def close(self):
        for copy in self.to_opp + self.to_sib + self.passed:
            copy.wait_send()


class Scatter:
    def __init__(self, stage, group, name, pieces, order=None):
        self.order = list(order or range(pieces))
        self.out_diag = stage[name + "_od"]
        self.out_sib = stage[name + "_os"]
        self.out_opp = stage[name + "_oo"]
        self.in_opp = stage[name + "_io"]
        self.in_own = stage[name + "_iw"]
        self.in_far = stage[name + "_if"]
        self.rows = self.out_diag.shape[0] // pieces
        base = stage.sems(3 * pieces, key=name)

        def copies(source, target, first, device):
            return [
                stage.remote(
                    source.at[self.part(s)], target.at[self.part(s)], base, first + s, {"tensor": device}
                )
                for s in range(pieces)
            ]

        self.first = copies(self.out_diag, self.in_opp, 0, group.sib)
        self.second = copies(self.out_sib, self.in_own, pieces, group.sib)
        self.across = copies(self.out_opp, self.in_far, 2 * pieces, group.opp)

    def part(self, s):
        return pl.ds(s * self.rows, self.rows)

    def put_diag(self, value, only=None):
        for s in self.order if only is None else [only]:
            self.out_diag[self.part(s), :] = value(s).astype(bf16)
            self.first[s].start()

    def put_opp(self, value, only=None):
        for s in self.order if only is None else [only]:
            mine = value(s)
            self.first[s].wait_recv()
            total = mine + self.in_opp[self.part(s), :].astype(f32)
            self.out_opp[self.part(s), :] = total.astype(bf16)
            self.across[s].start()

    def put_sib(self, value):
        self.fill_sib(value)
        self.send_sib()

    def fill_sib(self, value):
        for s in self.order:
            self.out_sib[self.part(s), :] = value(s).astype(bf16)

    def send_sib(self):
        for s in self.order:
            self.second[s].start()

    def take(self, s, own):
        self.second[s].wait_recv()
        near = own + self.in_own[self.part(s), :].astype(f32)
        self.across[s].wait_recv()
        return near + self.in_far[self.part(s), :].astype(f32)

    def close(self):
        for copy in self.first + self.second + self.across:
            copy.wait_send()


def pieces_of(value, count):
    rows = value.shape[0] // count
    return lambda s: value[s * rows : (s + 1) * rows]


def scatter_buffers(name, rows, width):
    return {
        name + tail: ((rows, width), bf16) for tail in ("_od", "_os", "_oo", "_io", "_iw", "_if")
    }


def ring_seats(count):
    index = lax.axis_index("dp")
    place = jnp.where(index % 2 == 0, index // 2, count - 1 - index // 2)

    def seat(p):
        p = lax.rem(p + 2 * count, count)
        return jnp.where(2 * p < count, 2 * p, 2 * (count - 1 - p) + 1)

    return place, seat


def ring_rows(shape, kind, count):
    tile = 16 if kind == bf16 else SUB
    if shape[0] % (2 * count * tile) == 0:
        return shape[0] // (2 * count), shape[1]
    if shape[0] % (count * tile) == 0 and shape[1] % (2 * LANES) == 0:
        return shape[0] // count, shape[1] // 2
    return None


class Ring:
    def __init__(self, m, count, items):
        self.m = m
        self.count = count
        self.items = items
        self.place, self.seat = ring_seats(count)
        self.steps = 2 * (count - 1)
        self.ahead = 0
        self.base = m.sems(len(items) * 2 * count, len(items) * 2)
        self.step = 0

    def neighbours(self):
        return self.seat(self.place - 1), self.seat(self.place + 1)

    def view(self, ref, chunk, way):
        shape = ref.shape
        rows, columns = ring_rows(shape, ref.dtype, self.count)
        chunk = lax.rem(chunk + 2 * self.count, self.count)
        if columns == shape[1]:
            return ref.at[pl.ds(pl.multiple_of((2 * chunk + way) * rows, rows), rows), :]
        return ref.at[
            pl.ds(pl.multiple_of(chunk * rows, rows), rows), pl.ds(way * columns, columns)
        ]

    def slot(self, item, way, step):
        own, box, _ = self.items[item]
        if len(box.shape) == 4:
            return box.at[way, step]
        rows, columns = ring_rows(own.shape, own.dtype, self.count)
        first = (way * (self.count - 1) + step) * rows
        return box.at[pl.ds(first, rows), pl.ds(0, columns)]

    def copy(self, item, way, step):
        own = self.items[item][0]
        sign = 1 - 2 * way
        last = self.count - 1
        place = 2 * item + way
        index = place * self.count + step % self.count
        if step < last:
            source = self.view(own, self.place, way) if step == 0 else self.slot(item, way, step - 1)
            target = self.slot(item, way, step)
        else:
            source = self.view(own, self.place + sign - sign * (step - last), way)
            target = source
        device = {"dp": self.seat(self.place + sign)}
        return self.m.remote(source, target, self.base, index, device, place)

    def start(self, item, way, step):
        self.copy(item, way, step).start()

    def begin(self):
        for item in range(len(self.items)):
            for way in range(2):
                self.start(item, way, 0)

    def tick(self):
        last = self.count - 1
        step = self.step
        self.step = step + 1
        for item, (own, _, name) in enumerate(self.items):
            for way in range(2):
                sign = 1 - 2 * way
                self.copy(item, way, step).wait_recv()
                self.copy(item, way, step).wait_send()
                if step < last:
                    chunk = self.view(own, self.place - sign * (step + 1), way)
                    box = self.slot(item, way, step)
                    value = box[...].astype(f32) + chunk[...].astype(f32)
                    if step < last - 1:
                        box[...] = value.astype(own.dtype)
                    else:
                        chunk[...] = value.astype(own.dtype)
                if step + 1 < self.steps:
                    self.start(item, way, step + 1)
                if step >= last - 1:
                    self.keep(own, name, self.place + sign - sign * (step + 1 - last), way)
        return step + 1 == self.steps

    def keep(self, own, name, chunk, way):
        out = self.m.hbm_out[name]
        sem = self.m.flush_sem.at[self.m.out_order[name]]
        pltpu.make_async_copy(self.view(own, chunk, way), self.view(out, chunk, way), sem).start()

    def close(self):
        for own, _, name in self.items:
            sem = self.m.flush_sem.at[self.m.out_order[name]]
            pltpu.make_async_copy(own, self.m.hbm_out[name], sem).wait()


class Direct:
    def __init__(self, m, count, items):
        self.m = m
        self.count = count
        self.items = items
        self.me = lax.axis_index("dp")
        self.base = m.sems(2 * len(items) * (count - 1))
        self.step = 0
        self.steps = 2
        self.ahead = 2 * count

    def share(self, ref, index):
        return ref.at[at(index, ref.shape[0] // self.count), :]

    def copies(self, step):
        made = []
        for item, (own, box, total, _) in enumerate(self.items):
            for r in range(1, self.count):
                there = lax.rem(self.me + r, self.count)
                index = (2 * item + step) * (self.count - 1) + r - 1
                if step == 0:
                    source, target = self.share(own, there), box.at[r - 1]
                else:
                    source = target = self.share(total, self.me)
                made.append(self.m.remote(source, target, self.base, index, {"dp": there}))
        return made

    def begin(self):
        for copy in self.copies(0):
            copy.start()

    def tick(self):
        for copy in self.copies(self.step):
            copy.wait_recv()
        if self.step == 0:
            for own, box, total, _ in self.items:
                value = self.share(own, self.me)[...].astype(f32)
                for r in range(self.count - 1):
                    value = value + box[r].astype(f32)
                self.share(total, self.me)[...] = value.astype(total.dtype)
            for copy in self.copies(1):
                copy.start()
        self.step += 1
        return self.step == 2

    def close(self):
        for copy in self.copies(0) + self.copies(1):
            copy.wait_send()
        for _, _, total, name in self.items:
            self.m.store(total, name)


class Turns:
    def __init__(self):
        self.waiting = []
        self.rings = []
        self.recent = []

    def begin(self, ring):
        ring.begin()
        self.waiting.append(ring)
        self.rings.append(ring)
        self.recent.append(ring)

    def tick(self, times=1):
        for _ in range(times):
            if self.waiting:
                recent = self.recent[-1:] if len(self.waiting) > 1 else []
                others = [ring for ring in self.waiting if ring not in recent]
                ring = max(others, key=lambda one: one.ahead + one.steps - one.step)
                self.recent.append(ring)
                if ring.tick():
                    self.waiting.remove(ring)

    def close(self):
        while self.waiting:
            self.tick()
        for ring in self.rings:
            ring.close()


def ring_box(shape, kind, count):
    rows, columns = ring_rows(shape, kind, count)
    return ((2, count - 1, rows, columns), kind)


def direct_box(shape, kind, count):
    return ((count - 1, shape[0] // count, shape[1]), kind)


def ring_fits(shapes, count):
    return (
        count > 1
        and count % 2 == 0
        and all(ring_rows(shape, kind, count) for shape, kind in shapes)
    )


def groups(array):
    halves = array.shape[0] // SUB
    sides = array.shape[1] // LANES
    return [
        array[SUB * s : SUB * s + SUB, LANES * l : LANES * l + LANES]
        for s in range(halves)
        for l in range(sides)
    ]


def spread_row(ref, index):
    return jnp.broadcast_to(ref[index], (SUB, LANES))


def advance(state, coefs, keep, signals, sides):
    root_real, root_imag = coefs
    half = len(state) // 2
    kept = [value * keep for value in state]
    fresh = [None] * len(state)
    for g in range(half):
        a_real, a_imag = kept[g], kept[half + g]
        fresh[g] = (root_real[g] * a_real - root_imag[g] * a_imag) + signals[g % sides]
        fresh[half + g] = root_real[g] * a_imag + root_imag[g] * a_real
    return kept, fresh


def filter_forward(m, first, count, state):
    sides = m.xl.shape[0]
    tables = m.tab
    root_real, root_imag = groups(tables[0]), groups(tables[1])
    out_real, out_imag = groups(tables[2]), groups(tables[3])
    half = len(root_real)
    unroll = 16

    def chunk(ch, state):
        for g in range(2 * half):
            m.st[ch, g] = state[g]

        def steps(i, state):
            state = list(state)
            for j in range(unroll):
                t = ch * SPAN + i * unroll + j
                keep = spread_row(m.kf, (pl.ds(t, 1), slice(None)))
                signals = [
                    spread_row(m.xl, (l, pl.ds(t, 1), slice(None))) for l in range(sides)
                ]
                _, state = advance(state, (root_real, root_imag), keep, signals, sides)
                for l in range(sides):
                    total = None
                    for g in range(l, half, sides):
                        term = out_real[g] * state[g] - out_imag[g] * state[half + g]
                        total = term if total is None else total + term
                    m.part[l, pl.ds(pl.multiple_of((i * unroll + j) * SUB, SUB), SUB), :] = total
            return tuple(state)

        state = lax.fori_loop(0, SPAN // unroll, steps, state)
        rows = at(ch, SPAN)
        for l in range(sides):
            lanes = slice(LANES * l, LANES * l + LANES)
            value = m.om[:, lanes] * m.xl[l, rows, :]
            for s in range(SUB):
                value = value + m.part[l, pl.ds(s, SPAN, stride=SUB), :]
            gate = sigmoid(value)
            m.mxl[rows, lanes] = (value * gate).astype(bf16)
            m.se[rows, lanes] = (gate * (1.0 + value * (1.0 - gate))).astype(bf16)
        return state

    return lax.fori_loop(first, first + count, chunk, state)


def window_mask(m, first_row, rows, first_key, keys):
    here = m.segb[pl.ds(pl.multiple_of(first_row + SUB, SUB), rows), :][:, :1]
    same = here == m.segr[:, pl.ds(pl.multiple_of(first_key, LANES), keys)].astype(f32)
    row = first_row + lax.broadcasted_iota(jnp.int32, (rows, keys), 0)
    key = first_key + lax.broadcasted_iota(jnp.int32, (rows, keys), 1)
    return same & (row >= key)


def window_of(index, block, length):
    back = -(-MAX_DOC // block)
    keys = min((back + 1) * block, length)
    first = jnp.maximum(index - back, 0) * block
    first = jnp.minimum(first, length - keys)
    return pl.multiple_of(first, LANES), keys


def keeping(m):
    length = m.segr.shape[1]
    m.segb[:SUB, :] = jnp.full((SUB, LANES), -1.0, f32)
    for k in range(length // LANES):
        row = m.segr[:, k * LANES : (k + 1) * LANES].astype(f32)
        m.segb[SUB + k * LANES : SUB + (k + 1) * LANES, :] = jnp.broadcast_to(row, (LANES, LANES)).T
    for k in range(length // LANES):
        now = m.segb[SUB + k * LANES : SUB + (k + 1) * LANES, :]
        before = m.segb[SUB - 1 + k * LANES : SUB - 1 + (k + 1) * LANES, :]
        m.kf[k * LANES : (k + 1) * LANES, :] = jnp.where(now == before, 1.0, 0.0)
    m.kf[length:, :] = jnp.zeros((SUB, LANES), f32)


def filter_tables(m):
    alpha, delta, theta, beta, e_re, e_im = (
        ref[...] for ref in (m.p0, m.p1, m.p2, m.p3, m.p4, m.p5)
    )
    magnitude = 1.0 - alpha * delta
    cosine, sine = jnp.cos(theta), jnp.sin(theta)
    scaled = alpha * beta
    entries = (
        magnitude * cosine, magnitude * sine, scaled * e_re, scaled * e_im,
        cosine, sine, alpha, delta, beta, e_re, e_im,
    )
    for k, entry in enumerate(entries):
        m.tab[k] = entry


def forward_attention(m, g):
    length, width = m.xt.shape
    block = m.tok.shape[0]
    blocks = length // block
    channels = m.mxl.shape[1]
    sides = channels // LANES
    own = at(g.me, block)
    half = block // 2
    tokens = Gather(
        m, g,
        lambda s: m.tok.at[pl.ds(s * half, half), :],
        lambda j, s: m.xt.at[pl.ds(pl.multiple_of(j * block + s * half, half), half), :],
        2, "rows",
    )
    shared = Gather(m, g, lambda s: m.wsh, lambda j, s: m.wsf.at[at(j, channels), :], 1)
    pieces = 8
    rows_piece = length // pieces
    mixed = Gather(
        m, g,
        lambda s: m.mxl.at[pl.ds(s * rows_piece, rows_piece), :],
        lambda j, s: m.mx.at[pl.ds(s * rows_piece, rows_piece), at(j, channels)],
        pieces,
    )
    cots = Gather(
        m, g,
        lambda s: m.cot.at[pl.ds(s * half, half), :],
        lambda j, s: m.cotf.at[pl.ds(pl.multiple_of(j * block + s * half, half), half), :],
        2,
    )
    normed = Gather(
        m, g,
        lambda s: m.yno.at[pl.ds(s * half, half), :],
        lambda j, s: m.yn.at[pl.ds(pl.multiple_of(j * block + s * half, half), half), :],
        2, "rows",
    )
    branch = Scatter(m, g, "xv", 2)

    m.need(m.tok, m.wsh)
    tokens.send(0)
    tokens.send(1)
    shared.send(0)
    m.need(m.cot)
    cots.send(0)
    m.xt[own, :] = m.tok[...]
    m.wsf[at(g.me, channels), :] = m.wsh[...]
    m.need(m.segr, m.p0, m.p1, m.p2, m.p3, m.p4, m.p5, m.gain, m.om)
    keeping(m)
    filter_tables(m)

    lane = lax.broadcasted_iota(jnp.int32, (SPAN, LANES), 1)

    def sums(j):
        def part(i, _):
            rows = pl.ds(pl.multiple_of(j * block + i * SPAN, SPAN), SPAN)
            one = jnp.zeros((SPAN, LANES), f32)
            two = jnp.zeros((SPAN, LANES), f32)
            for l in range(width // LANES):
                x = m.xt[rows, LANES * l : LANES * l + LANES].astype(f32)
                one = one + x
                two = two + x * x
            picked = jnp.where(lane == 6, 1.0, 0.0)
            for k, total in ((0, one), (3, two)):
                rest = jnp.sum(total, axis=1, keepdims=True)
                for n in range(3):
                    top = rest.astype(bf16).astype(f32)
                    picked = jnp.where(lane == k + n, top, picked)
                    rest = rest - top
            m.sums[rows, :] = picked.astype(bf16)
            return 0

        lax.fori_loop(0, block // SPAN, part, 0)

    sums(g.me)
    tokens.near()
    sums(g.sib)
    tokens.forward(0)
    tokens.forward(1)
    sums(g.opp)
    tokens.far()
    sums(g.diag)

    lane_wide = lax.broadcasted_iota(jnp.int32, (block, LANES), 1)

    def statistics(i, _):
        first, keys = window_of(i, block, length)
        seen = window_mask(m, i * block, block, first, keys).astype(bf16)
        got = plain(seen, m.sums[pl.ds(first, keys), :])
        pick = lambda low, high: jnp.sum(
            jnp.where((lane_wide >= low) & (lane_wide < high), got, 0.0), axis=1, keepdims=True
        )
        total = pick(6, 7) * width
        mean = pick(0, 3) / total
        var = pick(3, 6) / total - mean * mean
        rows = at(i, block)
        m.mean[rows, :] = jnp.broadcast_to(mean, (block, LANES))
        m.rstd[rows, :] = jnp.broadcast_to(lax.rsqrt(var + epsilon), (block, LANES))

        @pl.when(i == g.me)
        def _():
            m.so[0] = m.mean[rows, :]
            m.so[1] = m.rstd[rows, :]
            m.so[2] = jnp.broadcast_to(total, (block, LANES))

        return 0

    lax.fori_loop(0, blocks, statistics, 0)

    def normalise(i, _):
        rows = at(i, SPAN)
        mean, rstd = m.mean[rows, :], m.rstd[rows, :]
        for l in range(width // LANES):
            lanes = slice(LANES * l, LANES * l + LANES)
            x = m.xt[rows, lanes].astype(f32)
            m.xn[rows, lanes] = ((x - mean) * rstd * m.gain[:, lanes]).astype(bf16)
        for l in range(sides):
            lanes = pl.ds(pl.multiple_of(g.me * channels + LANES * l, LANES), LANES)
            x = m.xt[rows, lanes].astype(f32)
            m.xl[l, rows, :] = (x - mean) * rstd * m.gain[:, lanes]
        return 0

    lax.fori_loop(0, length // SPAN, normalise, 0)
    tokens.close()

    zero = jnp.zeros((SUB, LANES), f32)
    state = tuple(zero for _ in range(m.st.shape[1]))
    per = length // SPAN // pieces
    for p in range(pieces):
        state = filter_forward(m, p * per, per, state)
        mixed.send(p)
        if p >= 2:
            mixed.forward(p - 2)
    cots.send(1)
    for i in range(pieces):
        m.mx[pl.ds(i * rows_piece, rows_piece), at(g.me, channels)] = m.mxl[
            pl.ds(i * rows_piece, rows_piece), :
        ]
    m.cotf[own, :] = m.cot[...]
    m.need(m.wv)

    def values(i, _):
        rows = at(i, block)
        pre = plain(m.xn[rows, :], m.wv[...])
        gate = sigmoid(pre)
        m.v[rows, :] = (pre * gate).astype(bf16)
        m.sv[rows, :] = (gate * (1.0 + pre * (1.0 - gate))).astype(bf16)
        return 0

    lax.fori_loop(0, blocks, values, 0)
    for p in range(max(pieces - 2, 0), pieces):
        mixed.forward(p)
    shared.forward(0)
    shared.near()
    shared.far()
    mixed.near()
    mixed.far()
    m.need(m.qg, m.qb, m.kg, m.wag, m.wo, m.rg)

    def project(i, _):
        rows = at(i, block)
        z = plain(m.mx[rows, :], m.wsf[...])
        m.z[rows, :] = z.astype(bf16)
        m.q[rows, :] = (z * m.qg[...] + m.qb[...]).astype(bf16)
        m.k[rows, :] = (z * m.kg[...]).astype(bf16)
        return 0

    lax.fori_loop(0, blocks, project, 0)
    scale = 1.0 / math.sqrt(m.q.shape[1])

    def attend(i, part, count):
        size = block // count
        start = pl.multiple_of(i * block + part * size, size)
        rows = pl.ds(start, size)
        first, keys = window_of(i, block, length)
        window = pl.ds(first, keys)
        scores = cross(m.q[rows, :], m.k[window, :]) * scale
        scores = jnp.where(window_mask(m, start, size, first, keys), scores, masked_score)
        expo = jnp.exp(scores - jnp.max(scores, axis=1, keepdims=True))
        prob = (expo / jnp.sum(expo, axis=1, keepdims=True)).astype(bf16)
        m.p[i, pl.ds(part * size, size), :] = prob
        attended = plain(prob, m.v[window, :])
        pre = plain(m.mx[rows, :], m.wag[...])
        gate = sigmoid(pre)
        swish = pre * gate
        m.r[rows, :] = swish.astype(bf16)
        m.os[rows, :] = (attended * (gate * (1.0 + pre * (1.0 - gate)))).astype(bf16)
        m.w[rows, :] = (attended * swish).astype(bf16)
        return plain(m.w[rows, :], m.wo[...])

    for n in range(2):
        branch.put_diag(lambda s: attend(g.diag, s, 2), n)
        branch.put_opp(lambda s: attend(g.opp, s, 2), n)
    cots.forward(0)
    branch.put_sib(pieces_of(attend(g.sib, 0, 1), 2))
    cots.forward(1)
    m.bp[...] = attend(g.me, 0, 1)
    for s in range(2):
        piece = pl.ds(s * half, half)
        y = branch.take(s, m.bp[piece, :]) + m.tok[piece, :].astype(f32)
        m.y[piece, :] = y
        rms = lax.rsqrt(jnp.mean(y * y, axis=1, keepdims=True) + epsilon)
        m.rs[piece, :] = jnp.broadcast_to(rms, (half, LANES))
        m.yno[piece, :] = (y * rms * m.rg[...]).astype(bf16)
        normed.send(s)
    m.yn[own, :] = m.yno[...]
    for moved in (shared, mixed, branch):
        moved.close()
    return cots, normed


def transposed_product(left, right, out, step):
    def part(i, _):
        columns = at(i, step)
        out[columns, :] = inner(left[:, columns], right[...]).astype(bf16)
        return 0

    lax.fori_loop(0, left.shape[1] // step, part, 0)


def half_product(left, right, tokens, step, keep, done=None):
    def part(i, _):
        rows = at(i, step)
        value = inner(left[tokens, rows], right[tokens, :])
        keep(rows, value if done is None else value + done(rows))
        return 0

    lax.fori_loop(0, left.shape[1] // step, part, 0)


def strips(refs, width):
    size = refs[0].shape[1]
    spans = [(k * size, min((k + 1) * size, width)) for k in range(-(-width // size))]

    def store(rows, value):
        for ref, (low, high) in zip(refs, spans):
            ref[rows, : high - low] = value[:, low:high].astype(bf16)

    def load(rows):
        parts = [ref[rows, : high - low].astype(f32) for ref, (low, high) in zip(refs, spans)]
        return jnp.concatenate(parts, axis=1)

    return store, load


def feed_forward(m, g, cots, normed, turns, begin):
    length, width = m.yn.shape
    block = m.y.shape[0]
    half = block // 2
    grads = Scatter(m, g, "xv", 2)
    back = Gather(
        m, g,
        lambda s: m.dyo.at[pl.ds(s * half, half), :],
        lambda j, s: m.dyf.at[pl.ds(pl.multiple_of(j * block + s * half, half), half), :],
        2, "rows",
    )
    m.need(m.wg, m.wu, m.wd)

    def lead(j):
        rows = at(j, block)
        m.dg[rows, :] = cross(m.cotf[rows, :], m.wd[...]).astype(bf16)

    def feed(j):
        rows = at(j, block)
        low = m.yn[rows, :]
        gate = plain(low, m.wg[...])
        up = plain(low, m.wu[...])
        d_act = m.dg[rows, :].astype(f32)
        sig = sigmoid(gate)
        swish = gate * sig
        m.act[rows, :] = (swish * up).astype(bf16)
        m.dg[rows, :] = (d_act * up * (sig * (1.0 + gate * (1.0 - sig)))).astype(bf16)
        m.du[rows, :] = (d_act * swish).astype(bf16)
        return cross(m.dg[rows, :], m.wg[...]) + cross(m.du[rows, :], m.wu[...])

    lead(g.me)
    m.bp[...] = feed(g.me)
    cots.near()
    normed.near()
    lead(g.sib)
    grads.fill_sib(pieces_of(feed(g.sib), 2))
    normed.forward(0)
    cots.far()
    cots.close()
    lead(g.diag)
    lead(g.opp)
    chip = 2 * block
    near = at(g.me // 2, chip)
    far = at(1 - g.me // 2, chip)
    units = m.act.shape[1]

    def keep(ref):
        def store(rows, value):
            ref[rows, :] = value.astype(bf16)

        return store

    gate_store, gate_load = strips((m.dm_od, m.dm_os, m.dm_oo), units)
    up_store, up_load = strips((m.dm_io, m.dm_iw, m.dm_if), units)
    half_product(m.yn, m.dg, near, 2 * LANES, gate_store)
    half_product(m.yn, m.du, near, 2 * LANES, up_store)
    half_product(m.act, m.cotf, near, LANES, keep(m.gd))
    normed.forward(1)
    normed.far()
    grads.put_diag(pieces_of(feed(g.diag), 2))
    m.dy[...] = feed(g.opp)
    half_product(m.act, m.cotf, far, LANES, keep(m.gd), lambda rows: m.gd[rows, :].astype(f32))
    begin(0)
    grads.send_sib()
    grads.put_opp(lambda s: m.dy[pl.ds(s * half, half), :])
    half_product(m.yn, m.dg, far, 2 * LANES, keep(m.gg), gate_load)
    half_product(m.yn, m.du, far, 2 * LANES, keep(m.gu), up_load)
    begin(1)
    turns.tick(3)
    normed.close()
    m.need(m.y, m.rs, m.cot, m.rg)
    gain_sum = jnp.zeros((1, width), f32)
    for s in range(2):
        piece = pl.ds(s * half, half)
        d_yn = grads.take(s, m.bp[piece, :])
        rms = m.rs[piece, :][:, :1]
        hat = m.y[piece, :] * rms
        gain_sum = gain_sum + jnp.sum(d_yn * hat, axis=0, keepdims=True)
        d_hat = d_yn * m.rg[...]
        pull = d_hat - hat * jnp.mean(d_hat * hat, axis=1, keepdims=True)
        dy = m.cot[piece, :].astype(f32) + rms * pull
        m.dy[piece, :] = dy
        m.dyo[piece, :] = dy.astype(bf16)
        back.send(s)
    m.gr[...] = gain_sum
    m.dyf[at(g.me, block), :] = m.dyo[...]
    grads.close()
    return back


def filter_backward(m, last, count, gamma):
    sides = m.xl.shape[0]
    tables = m.tab
    root_real, root_imag = groups(tables[0]), groups(tables[1])
    out_real, out_imag = groups(tables[2]), groups(tables[3])
    half = len(root_real)
    unroll = 8

    def chunk(step, gamma):
        ch = last - step

        def again(i, state):
            state = list(state)
            for j in range(unroll):
                local = i * unroll + j
                t = ch * SPAN + local
                keep = spread_row(m.kf, (pl.ds(t, 1), slice(None)))
                signals = [
                    spread_row(m.xl, (l, pl.ds(t, 1), slice(None))) for l in range(sides)
                ]
                kept, state = advance(state, (root_real, root_imag), keep, signals, sides)
                for g in range(2 * half):
                    m.kept[local, g] = kept[g]
            return tuple(state)

        lax.fori_loop(0, SPAN // unroll, again, tuple(m.st[ch, g] for g in range(2 * half)))

        def reverse(i, carry):
            gamma, sums = list(carry[: 2 * half]), list(carry[2 * half :])
            for j in range(unroll):
                local = SPAN - 1 - (i * unroll + j)
                t = ch * SPAN + local
                keep = spread_row(m.kf, (pl.ds(t + 1, 1), slice(None)))
                signals = [
                    spread_row(m.dq, (l, pl.ds(t, 1), slice(None))) for l in range(sides)
                ]
                _, gamma = advance(gamma, (root_real, root_imag), keep, signals, sides)
                for l in range(sides):
                    total = None
                    for g in range(l, half, sides):
                        g_real, g_imag = gamma[g], gamma[half + g]
                        a_real, a_imag = m.kept[local, g], m.kept[local, half + g]
                        term = out_real[g] * g_real - out_imag[g] * g_imag
                        total = term if total is None else total + term
                        sums[g] = sums[g] + (g_real * a_real - g_imag * a_imag)
                        sums[half + g] = sums[half + g] + (g_real * a_imag + g_imag * a_real)
                        sums[2 * half + g] = sums[2 * half + g] + signals[l] * a_real
                        sums[3 * half + g] = sums[3 * half + g] + signals[l] * a_imag
                    m.part[l, pl.ds(pl.multiple_of(local * SUB, SUB), SUB), :] = total
            return tuple(gamma) + tuple(sums)

        start = tuple(gamma) + tuple(m.acc[g] for g in range(4 * half))
        done = lax.fori_loop(0, SPAN // unroll, reverse, start)
        for g in range(4 * half):
            m.acc[g] = done[2 * half + g]
        rows = at(ch, SPAN)
        for l in range(sides):
            lanes = slice(LANES * l, LANES * l + LANES)
            signal = m.dq[l, rows, :]
            value = m.om[:, lanes] * signal
            for s in range(SUB):
                value = value + m.part[l, pl.ds(s, SPAN, stride=SUB), :]
            m.dxb[rows, lanes] = value.astype(bf16)
            m.go[:, lanes] = m.go[:, lanes] + jnp.sum(
                signal * m.xl[l, rows, :], axis=0, keepdims=True
            )
        return done[: 2 * half]

    return lax.fori_loop(0, count, chunk, gamma)


def filter_gradients(m):
    sides = m.xl.shape[0]
    half = m.acc.shape[0] // 4
    dims = m.tab.shape[1]
    for g in range(half):
        s, l = g // sides, g % sides
        rows = slice(SUB * s, SUB * s + SUB)
        lanes = slice(LANES * l, LANES * l + LANES)
        q_re, q_im, c_re, c_im, cosine, sine, alpha, delta, beta, e_re, e_im = (
            m.tab[k, rows, lanes] for k in range(11)
        )
        lag_re, lag_im, sum_re, sum_im = (m.acc[k * half + g] for k in range(4))
        f_re = q_re * sum_re - q_im * sum_im + m.go[:, lanes]
        f_im = q_re * sum_im + q_im * sum_re
        scaled = alpha * beta
        d_scaled = e_re * f_re - e_im * f_im
        w_re = c_re * lag_re - c_im * lag_im
        w_im = c_re * lag_im + c_im * lag_re
        d_mag = w_re * cosine - w_im * sine
        m.pk[0 * dims + SUB * s : 0 * dims + SUB * s + SUB, lanes] = beta * d_scaled - delta * d_mag
        m.pk[1 * dims + SUB * s : 1 * dims + SUB * s + SUB, lanes] = -alpha * d_mag
        m.pk[2 * dims + SUB * s : 2 * dims + SUB * s + SUB, lanes] = -(w_re * q_im + w_im * q_re)
        m.pk[3 * dims + SUB * s : 3 * dims + SUB * s + SUB, lanes] = alpha * d_scaled
        m.pk[4 * dims + SUB * s : 4 * dims + SUB * s + SUB, lanes] = scaled * f_re
        m.pk[5 * dims + SUB * s : 5 * dims + SUB * s + SUB, lanes] = -scaled * f_im


def backward_attention(m, g, back, turns, begin):
    length, width = m.mx.shape
    block = m.tok.shape[0]
    blocks = length // block
    half = block // 2
    channels = m.se.shape[1]
    shared = m.q.shape[1]
    sides = channels // LANES
    fed = Scatter(m, g, "xv", 2)
    pieces = 4
    dm = Scatter(m, g, "dm", pieces, range(pieces - 1, -1, -1))
    sh = Scatter(m, g, "sh", 1)
    others = (g.sib, g.opp, g.diag)
    base = m.sems(9)
    parts = [
        m.remote(m.dxb.at[at(dev, block), :], m.dxr.at[k], base, k, {"tensor": dev})
        for k, dev in enumerate(others)
    ]
    small = [
        m.remote(m.smo, m.sm.at[g.me], base, 3 + k, {"tensor": dev})
        for k, dev in enumerate(others)
    ]
    tails = [
        m.remote(m.aro, m.ar.at[:, at(g.me, block)], base, 6 + k, {"tensor": dev})
        for k, dev in enumerate(others)
    ]

    scale = 1.0 / math.sqrt(shared)
    m.dk[...] = jnp.zeros(m.dk.shape, f32)
    m.dv[...] = jnp.zeros(m.dv.shape, f32)
    turns.tick(2)
    back.forward(0)
    turns.tick(2)
    back.forward(1)
    back.near()
    back.far()
    share = lambda j: plain(m.act[at(j, block), :], m.wd[...])
    fed.put_diag(pieces_of(share(g.diag), 2))
    turns.tick()
    fed.put_opp(pieces_of(share(g.opp), 2))
    turns.tick()
    fed.put_sib(pieces_of(share(g.sib), 2))
    m.bp[...] = share(g.me)
    m.need(m.w, m.wo, m.r, m.os, m.v, m.p, m.k, m.q)
    transposed_product(m.w, m.dyf, m.gao, 2 * LANES)
    turns.tick()

    def attend(i, _):
        rows = at(i, block)
        first, keys = window_of(i, block, length)
        window = pl.ds(first, keys)
        d_w = cross(m.dyf[rows, :], m.wo[...])
        d_o = (d_w * m.r[rows, :].astype(f32)).astype(bf16)
        m.drp[rows, :] = (d_w * m.os[rows, :].astype(f32)).astype(bf16)
        prob_low = m.p[i]
        prob = prob_low.astype(f32)
        weighed = prob * cross(d_o, m.v[window, :])
        d_s = (weighed - prob * jnp.sum(weighed, axis=1, keepdims=True)) * scale
        d_s = d_s.astype(bf16)
        d_q = plain(d_s, m.k[window, :])
        for l in range(shared // LANES):
            m.dq[l, rows, :] = d_q[:, LANES * l : LANES * l + LANES]
        m.dk[window, :] = m.dk[window, :] + inner(d_s, m.q[rows, :])
        m.dv[window, :] = m.dv[window, :] + inner(prob_low, d_o)
        return 0

    for n in range(blocks):
        attend(n, 0)
        turns.tick()
    m.need(m.z, m.qg, m.kg, m.sv, m.wsf, m.wag)

    def affine(i, sums):
        rows = at(i, block)
        d_q = jnp.concatenate([m.dq[l, rows, :] for l in range(shared // LANES)], axis=1)
        d_k, z = m.dk[rows, :], m.z[rows, :].astype(f32)
        m.dz[rows, :] = (d_q * m.qg[...] + d_k * m.kg[...]).astype(bf16)
        m.dvp[rows, :] = (m.dv[rows, :] * m.sv[rows, :].astype(f32)).astype(bf16)
        new = (d_q * z, d_q, d_k * z)
        return tuple(s + jnp.sum(n, axis=0, keepdims=True) for s, n in zip(sums, new))

    aff = lax.fori_loop(0, blocks, affine, tuple(jnp.zeros((1, shared), f32) for _ in range(3)))
    m.smo[...] = jnp.zeros(m.smo.shape, f32)
    for n in range(3):
        m.smo[2 + n : 3 + n, :shared] = aff[n]

    def mixing(j):
        def value(s):
            rows = pl.ds(s * (length // pieces), length // pieces)
            return cross(m.dz[rows, :], m.wsf[at(j, channels), :]) + cross(
                m.drp[rows, :], m.wag[at(j, channels), :]
            )

        return value

    m.need(m.y)
    for s in range(2):
        piece = pl.ds(s * half, half)
        m.out[piece, :] = (fed.take(s, m.bp[piece, :]) + m.y[piece, :]).astype(bf16)
    m.flush(m.out)
    fed.close()
    turns.tick()
    m.need(m.mx, m.xn)
    transposed_product(m.mx, m.drp, m.r, 2 * LANES)
    turns.tick()
    transposed_product(m.xn, m.dvp, m.os, 2 * LANES)
    begin(2)
    dm.put_diag(mixing(g.diag))
    turns.tick()
    dm.put_opp(mixing(g.opp))
    turns.tick()
    dm.put_sib(mixing(g.sib))
    turns.tick()
    m.need(m.wv)
    xv = Scatter(m, g, "xv", 2)
    spread = lambda j: pieces_of(cross(m.dvp[at(j, block), :], m.wv[...]), 2)
    split = lambda j: (lambda s: inner(m.mx[:, at(j, channels)], m.dz[...]))

    def spreading():
        xv.put_diag(spread(g.diag))
        xv.put_opp(spread(g.opp))
        turns.tick()
        xv.put_sib(spread(g.sib))
        m.bp[...] = cross(m.dvp[at(g.me, block), :], m.wv[...])
        turns.tick()
        sh.put_diag(split(g.diag))
        sh.put_opp(split(g.opp))
        turns.tick()
        sh.put_sib(split(g.sib))
        m.shp[...] = split(g.me)(0)
        turns.tick()

    m.need(m.se, m.st, m.xl, m.kf, m.tab, m.om)
    half_states = m.acc.shape[0] // 4
    m.acc[...] = jnp.zeros(m.acc.shape, f32)
    m.go[...] = jnp.zeros(m.go.shape, f32)
    gamma = tuple(jnp.zeros((SUB, LANES), f32) for _ in range(2 * half_states))
    per = length // SPAN // pieces
    own_mix = mixing(g.me)
    for s in range(pieces - 1, -1, -1):
        rows = pl.ds(s * (length // pieces), length // pieces)
        d_e = dm.take(s, own_mix(s)) * m.se[rows, :].astype(f32)
        for l in range(sides):
            m.dq[l, rows, :] = d_e[:, LANES * l : LANES * l + LANES]
        for n in range(per - 1, -1, -2):
            gamma = filter_backward(m, s * per + n, 2, gamma)
            turns.tick(2)
        for k, dev in enumerate(others):

            @pl.when(dev == s)
            def _():
                parts[k].start()

        if s == pieces - 1:
            spreading()
    filter_gradients(m)
    base_row = m.pk.shape[0] - PACK_TAIL
    m.pk[base_row:, :] = jnp.zeros((PACK_TAIL, channels), f32)
    m.pk[base_row : base_row + 1, :] = m.go[...]
    m.gs[...] = sh.take(0, m.shp[...]).astype(bf16)
    turns.tick()
    m.need(m.tok, m.so, m.gain, m.dy, m.gr, m.segb, m.segr)
    for s in range(2):
        piece = pl.ds(s * half, half)
        m.bp[piece, :] = xv.take(s, m.bp[piece, :])
    own_columns = at(g.me, channels)
    m.bp[:, own_columns] = m.bp[:, own_columns] + m.dxb[at(g.me, block), :].astype(f32)
    for k, dev in enumerate(others):
        parts[k].wait_recv()
        columns = at(dev, channels)
        m.bp[:, columns] = m.bp[:, columns] + m.dxr[k].astype(f32)
    gain_sum = jnp.zeros((1, width), f32)
    lane = lax.broadcasted_iota(jnp.int32, (half, LANES), 1)
    for s in range(2):
        piece = pl.ds(s * half, half)
        mean, rstd, total = (m.so[n, piece, :][:, :1] for n in range(3))
        centred = m.tok[piece, :].astype(f32) - mean
        d_xn = m.bp[piece, :]
        gain_sum = gain_sum + jnp.sum(d_xn * (centred * rstd), axis=0, keepdims=True)
        d_hat = d_xn * m.gain[...]
        d_var = -0.5 * rstd * rstd * rstd * jnp.sum(d_hat * centred, axis=1, keepdims=True)
        one = (-rstd * jnp.sum(d_hat, axis=1, keepdims=True) - 2.0 * mean * d_var) / total
        two = d_var / total
        m.bp[piece, :] = d_hat * rstd + m.dy[piece, :]
        m.aw[piece, :] = jnp.where(lane == 0, one, jnp.where(lane == 1, two, 0.0))
    m.smo[0:1, :] = gain_sum
    m.smo[1:2, :] = m.gr[...]
    turned = m.aw[...].T
    for n in range(2):
        rest = turned[n : n + 1, :]
        for k in range(3):
            top = rest.astype(bf16).astype(f32)
            m.art[3 * n + k : 3 * n + k + 1, :] = top
            rest = rest - top
    m.art[6:8, :] = jnp.zeros((2, block), f32)
    m.art[8:16, :] = jnp.zeros((8, block), f32)
    m.aro[...] = m.art[...].astype(bf16)
    for copy in tails + small:
        copy.start()
    m.ar[:, at(g.me, block)] = m.aro[...]
    m.sm[g.me] = m.smo[...]
    reach = -(-MAX_DOC // block)
    keys = min((reach + 1) * block, length)
    first_key = pl.multiple_of(jnp.minimum(g.me * block, length - keys), LANES)
    first_row = pl.multiple_of(g.me * block, LANES)
    here = m.segb[pl.ds(pl.multiple_of(first_row + SUB, SUB), block), :][:, :1]
    same = here == m.segr[:, pl.ds(first_key, keys)].astype(f32)
    row = first_row + lax.broadcasted_iota(jnp.int32, (block, keys), 0)
    key = first_key + lax.broadcasted_iota(jnp.int32, (block, keys), 1)
    seen = (same & (row <= key)).astype(bf16)
    for copy in tails:
        copy.wait_recv()
    pulled = cross(seen, m.ar[:, pl.ds(first_key, keys)])
    b_one = pulled[:, 0:1] + pulled[:, 1:2] + pulled[:, 2:3]
    b_two = pulled[:, 3:4] + pulled[:, 4:5] + pulled[:, 5:6]
    for s in range(2):
        piece = pl.ds(s * half, half)
        rows = slice(s * half, (s + 1) * half)
        x = m.tok[piece, :].astype(f32)
        m.gt[piece, :] = (m.bp[piece, :] + b_one[rows] + 2.0 * x * b_two[rows]).astype(bf16)
    m.flush(m.gt)
    turns.tick()
    for copy in small:
        copy.wait_recv()
    total = m.sm[0]
    for j in range(1, m.sm.shape[0]):
        total = total + m.sm[j]
    per = width // channels
    for n in range(2):
        for k in range(per):
            row = base_row + 1 + n * per + k
            m.pk[row : row + 1, :] = total[n : n + 1, k * channels : (k + 1) * channels]
    for n in range(3):
        row = base_row + 1 + 2 * per + n
        m.pk[row : row + 1, :shared] = total[2 + n : 3 + n, :shared]
    begin(3)
    turns.close()
    for moved in (dm, xv, sh, back):
        moved.close()
    for copy in parts + small + tails:
        copy.wait_send()


def body(count, m):
    g = Group()
    m.load(m.tok, m.wsh, m.cot, m.segr, m.p0, m.p1, m.p2, m.p3, m.p4, m.p5)
    m.load(m.gain, m.om, m.wv, m.wag, m.qg, m.qb, m.kg, m.wo, m.rg, m.wg, m.wu, m.wd)
    m.refs.update(mean=m.dq.at[0], rstd=m.dq.at[1])
    turns = Turns()
    plans = (
        [(m.gd, m.gdb, "gdt")],
        [(m.gg, m.ggb, "ggt"), (m.gu, m.gub, "gut")],
        [(m.gao, m.gaob, "gaot"), (m.r, m.gagb, "gagt"), (m.os, m.gvb, "gvt")],
    ) if count else ()
    rings = [Ring(m, count, plan) for plan in plans]
    if count:
        rings.append(Direct(m, count, [(m.gs, m.gsb, m.gss, "gst"), (m.pk, m.pkb, m.pks, "pkt")]))
        g.greet(rings[0].neighbours())
    else:
        g.greet()

    alone = (
        ((m.gd, "gdt"),),
        ((m.gg, "ggt"), (m.gu, "gut")),
        ((m.gao, "gaot"), (m.r, "gagt"), (m.os, "gvt")),
        ((m.gs, "gst"), (m.pk, "pkt")),
    )

    def begin(n):
        if rings:
            turns.begin(rings[n])
        else:
            for ref, name in alone[n]:
                m.store(ref, name)

    cots, normed = forward_attention(m, g)
    back = feed_forward(m, g, cots, normed, turns, begin)
    backward_attention(m, g, back, turns, begin)
    m.close()


def run(arrays, sizes, count):
    length, width, block, channels, shared, values, units = sizes
    blocks = length // block
    keys = min((-(-MAX_DOC // block) + 1) * block, length)
    sides = channels // LANES
    dims = arrays.p0.shape[0]
    half_states = sides * (dims // SUB)
    late = dict(
        gao=((values, width), bf16),
        gag=((width, values), bf16),
        gv=((width, values), bf16),
        gs=((channels, shared), bf16),
        pk=((6 * dims + PACK_TAIL, channels), f32),
    )
    summed = dict(
        gd=((units, width), bf16),
        gg=((width, units), bf16),
        gu=((width, units), bf16),
        **late,
    )
    if not ring_fits(summed.values(), count):
        count = 0
    outs = dict(
        gt=((block, width), bf16),
        out=((block, width), bf16),
    )
    scratch = dict(
        xt=((length, width), bf16),
        cotf=((length, width), bf16),
        xn=((length, width), bf16),
        mx=((length, width), bf16),
        xl=((sides, length, LANES), f32),
        tab=((11, dims, channels), f32),
        kf=((length + SUB, LANES), f32),
        segb=((length + SUB, LANES), f32),
        so=((3, block, LANES), f32),
        sums=((length, LANES), bf16),
        se=((length, channels), bf16),
        st=((length // SPAN, 2 * half_states, SUB, LANES), f32),
        v=((length, values), bf16),
        sv=((length, values), bf16),
        z=((length, shared), bf16),
        q=((length, shared), bf16),
        k=((length, shared), bf16),
        wsf=((width, shared), bf16),
        p=((blocks, block, keys), bf16),
        r=((length, values), bf16),
        os=((length, values), bf16),
        w=((length, values), bf16),
        y=((block, width), f32),
        rs=((block, LANES), f32),
        yno=((block, width), bf16),
        bp=((block, width), f32),
        act=((length, units), bf16),
        dg=((length, units), bf16),
        du=((length, units), bf16),
        gd=summed["gd"],
        dy=((block, width), f32),
        gr=((1, width), f32),
        dk=((length, shared), f32),
        dv=((length, values), f32),
        dq=((max(sides, shared // LANES), length, LANES), f32),
        shp=((channels, shared), f32),
        go=((1, channels), f32),
        acc=((4 * half_states, SUB, LANES), f32),
        kept=((SPAN, 2 * half_states, SUB, LANES), f32),
        part=((sides, SPAN * SUB, LANES), f32),
        dxr=((3, block, channels), bf16),
        art=((16, block), f32),
        aro=((16, block), bf16),
        ar=((16, length), bf16),
        smo=((SUB, width), f32),
        sm=((length // block, SUB, width), f32),
        gao=late["gao"],
        gs=late["gs"],
        pk=late["pk"],
        **scatter_buffers("dm", length, channels),
        **scatter_buffers("xv", block, width),
        **scatter_buffers("sh", channels, shared),
    )
    alias = dict(yn="xt", dyf="cotf", gg="wg", gu="wu", dyo="yno", dvp="v", aw="rs")
    alias.update(dz="q", dxb="k", drp="w", mxl="dm_os")
    shared_boxes = dict(gag="dg", gv="du")
    sems = [69, 69]
    if count:
        for name, (shape, kind) in summed.items():
            small = name in ("gs", "pk")
            used = count - 1, *(ring_rows(shape, kind, count) or ())
            if name in shared_boxes and 2 * used[0] * used[1] <= length and used[2] <= units:
                alias[name + "b"] = shared_boxes[name]
                continue
            scratch[name + "b"] = (direct_box if small else ring_box)(shape, kind, count)
        scratch.update(gss=summed["gs"], pks=summed["pk"])
        sems = [69 + 12 + 4 * (count - 1), 69 + 12 * count + 4 * (count - 1)]
    bare = {name + "t": entry for name, entry in summed.items()}
    done = run_stage(
        functools.partial(body, count), arrays, outs, scratch, sems, 1, bare.items(), alias.items()
    )
    done.dims = dims
    done.summed = bool(count)
    return done


def body_f(dims, shared, m):
    wide = ((m.gd, m.gdt), (m.gg, m.ggt), (m.gu, m.gut), (m.gao, m.gaot), (m.gag, m.gagt))
    wide += ((m.gv, m.gvt), (m.gs, m.gst))
    m.load(m.out, m.gt, m.gd, m.gg, m.gu, m.gao, m.gag, m.gv, m.gs, m.pk)
    for source, target in ((m.out, m.outt), (m.gt, m.gtt)):
        m.need(source)
        target[...] = source[...]
        m.flush(target)
    for source, target in wide:
        m.need(source)
        rows = source.shape[0] // 2
        for n in range(2):

            def part(i, _):
                piece = pl.ds(pl.multiple_of(n * rows + i * 16, 16), 16)
                target[piece, :] = source[piece, :].astype(f32)
                return 0

            lax.fori_loop(0, rows // 16, part, 0, unroll=4)
        m.flush(target)
    m.need(m.pk)
    for k, out in enumerate((m.e0, m.e1, m.e2, m.e3, m.e4, m.e5)):
        out[...] = m.pk[k * dims : (k + 1) * dims, :]
    top = 6 * dims
    channels = m.pk.shape[1]
    m.om[...] = m.pk[top : top + 1, :]
    per = m.norm.shape[1] // channels
    for n, out in enumerate((m.norm, m.rms)):
        for k in range(per):
            row = top + 1 + n * per + k
            out[:, k * channels : (k + 1) * channels] = m.pk[row : row + 1, :]
    for n, out in enumerate((m.qg, m.qb, m.kg)):
        row = top + 1 + 2 * per + n
        out[...] = m.pk[row : row + 1, :shared]
    m.flush(m.e0, m.e1, m.e2, m.e3, m.e4, m.e5, m.om, m.norm, m.rms, m.qg, m.qb, m.kg)
    m.close()


def finish(c, shared):
    sums = dict(gd=c.gdt, gg=c.ggt, gu=c.gut, gao=c.gaot, gag=c.gagt, gv=c.gvt, gs=c.gst, pk=c.pkt)
    if not c.summed:
        total = lax.psum([value.astype(f32) for value in sums.values()], "dp")
        sums = {name: v.astype(old.dtype) for (name, old), v in zip(sums.items(), total)}
    channels, width = sums["pk"].shape[1], sums["gd"].shape[1]
    outs = dict(
        e0=((c.dims, channels), f32),
        e1=((c.dims, channels), f32),
        e2=((c.dims, channels), f32),
        e3=((c.dims, channels), f32),
        e4=((c.dims, channels), f32),
        e5=((c.dims, channels), f32),
        om=((1, channels), f32),
        norm=((1, width), f32),
        rms=((1, width), f32),
        qg=((1, shared), f32),
        qb=((1, shared), f32),
        kg=((1, shared), f32),
    )
    for name, value in sums.items():
        if value is not sums["pk"]:
            outs[name + "t"] = (value.shape, f32)
    outs.update(outt=(c.out.shape, bf16), gtt=(c.gt.shape, bf16))
    f = run_stage(
        functools.partial(body_f, c.dims, shared),
        types.SimpleNamespace(out=c.out, gt=c.gt, **sums), outs, {}, (0, 0), None,
    )
    tables = [table.T for table in (f.e0, f.e1, f.e2, f.e3, f.e4, f.e5)]
    return (
        f.outt, f.gtt, f.norm[0], *tables, f.om[0], f.gst,
        f.qg[0], f.qb[0], f.kg[0], f.gagt, f.gvt, f.gaot, f.rms[0], f.ggt, f.gut, f.gdt,
    )


def on_device(
    tokens,
    segments,
    cotangent,
    timestep_norm_gain,
    ema_alpha,
    ema_delta,
    ema_theta,
    ema_beta,
    eta_real,
    eta_imag,
    ema_omega,
    w_shared,
    q_gain,
    q_bias,
    k_gain,
    w_attgate,
    w_value,
    w_attout,
    rms_gain,
    w_gate,
    w_up,
    w_down,
):
    block, width = tokens.shape
    length = segments.shape[1]
    channels, dims = ema_alpha.shape
    shared = w_shared.shape[1]
    values = w_value.shape[1]
    units = w_gate.shape[1]
    om = ema_omega[None]
    gain, rg = timestep_norm_gain[None], rms_gain[None]
    qg, qb, kg = q_gain[None], q_bias[None], k_gain[None]
    segr = segments
    done = run(
        types.SimpleNamespace(
            tok=tokens, cot=cotangent, wsh=w_shared, segr=segr, gain=gain,
            p0=ema_alpha.T, p1=ema_delta.T, p2=ema_theta.T,
            p3=ema_beta.T, p4=eta_real.T, p5=eta_imag.T, om=om, qg=qg, qb=qb, kg=kg,
            wag=w_attgate, wv=w_value, wo=w_attout, rg=rg, wg=w_gate, wu=w_up, wd=w_down,
        ),
        (length, width, block, channels, shared, values, units),
        lax.axis_size("dp"),
    )
    return finish(done, shared)


def solution(mesh):
    placed = (
        P(("dp", "tensor"), None),
        P("dp", None),
        P(("dp", "tensor"), None),
        P(),
        P("tensor", None),
        P("tensor", None),
        P("tensor", None),
        P("tensor", None),
        P("tensor", None),
        P("tensor", None),
        P("tensor"),
        P("tensor", None),
        P(),
        P(),
        P(),
        P(None, "tensor"),
        P(None, "tensor"),
        P("tensor", None),
        P(),
        P(None, "tensor"),
        P(None, "tensor"),
        P("tensor", None),
    )
    return jax.shard_map(
        on_device,
        mesh=mesh,
        in_specs=placed,
        out_specs=(
            P(("dp", "tensor"), None),
            P(("dp", "tensor"), None),
            P(),
            P("tensor", None),
            P("tensor", None),
            P("tensor", None),
            P("tensor", None),
            P("tensor", None),
            P("tensor", None),
            P("tensor"),
            P("tensor", None),
            P(),
            P(),
            P(),
            P(None, "tensor"),
            P(None, "tensor"),
            P("tensor", None),
            P(),
            P(None, "tensor"),
            P(None, "tensor"),
            P("tensor", None),
        ),
        check_vma=False,
    )
```

profile of v0, /device:TPU:0, one launch (start us, length us, event | category | flops | bytes accessed | tf_op | source)
XLA Modules:
  0.0 242.0 jit_solution(75350629868457199)
XLA Ops:
  0.7 233.1 %shard_map.373 = (bf16[256,1024]{1,0:T(8,128)(2,1)}, bf16[256,1024]{1,0:T(8,128)(2,1)}, bf16[640,1024]{1,0:T(8,128)(2,1)}, bf16[1024,640]{1,0:T(8,128)(2,1)}, bf...) custom-call(bf16[256,1024]{1,0:T(8,128)(2,1)} %refs_0_.1, ...), custom_call_target="tpu_custom_call" | custom-call | tf_op jit(solution)/shard_map/pallas_call | solution.py:139
  233.8 7.9 %shard_map.374 = (f32[16,256]{1,0:T(8,128)}, f32[16,256]{1,0:T(8,128)}, f32[16,256]{1,0:T(8,128)}, f32[16,256]{1,0:T(8,128)}, f32[16,256]{1,0:T(8,128)}, /*index...) custom-call(bf16[256,1024]{1,0:T(8,128)(2,1)} %get-tuple-element.52., ...), custom_call_target="tpu_custom_call" | custom-call | tf_op jit(solution)/shard_map/pallas_call | solution.py:139
where the time goes:
time: 246 us; the launch traced here: 242 us
  Pallas kernels  241 us (98%)
    pallas_call x2, Pallas kernels, run_stage(): pl.pallas_call(kernel, out_shape=tuple((jax.ShapeDtypeStruct(shape, kind)...  241 us

commit v1 on v0

--- a/solution.py
+++ b/solution.py
@@ -316,7 +316,7 @@
         self.items = items
         self.place, self.seat = ring_seats(count)
         self.steps = 2 * (count - 1)
-        self.ahead = 0
+        self.ahead = self.pause = 0
         self.base = m.sems(len(items) * 2 * count, len(items) * 2)
         self.step = 0
 
@@ -408,6 +408,7 @@
         self.step = 0
         self.steps = 2
         self.ahead = 2 * count
+        self.pause = 3
 
     def share(self, ref, index):
         return ref.at[at(index, ref.shape[0] // self.count), :]
@@ -465,8 +466,8 @@
     def tick(self, times=1):
         for _ in range(times):
             if self.waiting:
-                recent = self.recent[-1:] if len(self.waiting) > 1 else []
-                others = [ring for ring in self.waiting if ring not in recent]
+                others = [one for one in self.waiting if one not in self.recent[-1 - one.pause :]]
+                others = others or [one for one in self.waiting if not one.pause] or self.waiting
                 ring = max(others, key=lambda one: one.ahead + one.steps - one.step)
                 self.recent.append(ring)
                 if ring.tick():
@@ -1186,7 +1187,7 @@
             m.dq[l, rows, :] = d_e[:, LANES * l : LANES * l + LANES]
         for n in range(per - 1, -1, -2):
             gamma = filter_backward(m, s * per + n, 2, gamma)
-            turns.tick(2)
+            turns.tick()
         for k, dev in enumerate(others):
 
             @pl.when(dev == s)

time: 246 us -> 241 us (0.980)
  Pallas kernels: 241 us -> 237 us
    pallas_call x2, Pallas kernels: 241 us -> 237 us  [run_stage(): pl.pallas_call(kernel, out_shape=tuple((jax.ShapeDtypeStruct(shape, kind)...]
where the time goes in v1:
time: 241 us; the launch traced here: 238 us
  Pallas kernels  237 us (98%)
    pallas_call x2, Pallas kernels, run_stage(): pl.pallas_call(kernel, out_shape=tuple((jax.ShapeDtypeStruct(shape, kind)...  237 us

profile of v1, /device:TPU:0, one launch (start us, length us, event | category | flops | bytes accessed | tf_op | source)
XLA Modules:
  0.0 237.8 jit_solution(11658002497638732206)
XLA Ops:
  0.7 228.9 %shard_map.373 = (bf16[256,1024]{1,0:T(8,128)(2,1)}, bf16[256,1024]{1,0:T(8,128)(2,1)}, bf16[640,1024]{1,0:T(8,128)(2,1)}, bf16[1024,640]{1,0:T(8,128)(2,1)}, bf...) custom-call(bf16[256,1024]{1,0:T(8,128)(2,1)} %refs_0_.1, ...), custom_call_target="tpu_custom_call" | custom-call | tf_op jit(solution)/shard_map/pallas_call | solution.py:139
  229.6 7.9 %shard_map.374 = (f32[16,256]{1,0:T(8,128)}, f32[16,256]{1,0:T(8,128)}, f32[16,256]{1,0:T(8,128)}, f32[16,256]{1,0:T(8,128)}, f32[16,256]{1,0:T(8,128)}, /*index...) custom-call(bf16[256,1024]{1,0:T(8,128)(2,1)} %get-tuple-element.52., ...), custom_call_target="tpu_custom_call" | custom-call | tf_op jit(solution)/shard_map/pallas_call | solution.py:139

commit v2 on v1

--- a/solution.py
+++ b/solution.py
@@ -19,6 +19,7 @@
 SPAN = 64
 MAX_DOC = 512
 PACK_TAIL = 32
+RING_SLOTS = 4
 VMEM_BYTES = 62 * 2**20
 
 
@@ -317,7 +318,7 @@
         self.place, self.seat = ring_seats(count)
         self.steps = 2 * (count - 1)
         self.ahead = self.pause = 0
-        self.base = m.sems(len(items) * 2 * count, len(items) * 2)
+        self.base = m.sems(len(items) * 2 * RING_SLOTS, len(items) * 2)
         self.step = 0
 
     def neighbours(self):
@@ -346,7 +347,7 @@
         sign = 1 - 2 * way
         last = self.count - 1
         place = 2 * item + way
-        index = place * self.count + step % self.count
+        index = place * RING_SLOTS + step % RING_SLOTS
         if step < last:
             source = self.view(own, self.place, way) if step == 0 else self.slot(item, way, step - 1)
             target = self.slot(item, way, step)
@@ -1072,7 +1073,7 @@
     scale = 1.0 / math.sqrt(shared)
     m.dk[...] = jnp.zeros(m.dk.shape, f32)
     m.dv[...] = jnp.zeros(m.dv.shape, f32)
-    turns.tick(2)
+    turns.tick(3)
     back.forward(0)
     turns.tick(2)
     back.forward(1)
@@ -1415,7 +1416,7 @@
                 continue
             scratch[name + "b"] = (direct_box if small else ring_box)(shape, kind, count)
         scratch.update(gss=summed["gs"], pks=summed["pk"])
-        sems = [69 + 12 + 4 * (count - 1), 69 + 12 * count + 4 * (count - 1)]
+        sems = [69 + 12 + 4 * (count - 1), 69 + 12 * RING_SLOTS + 4 * (count - 1)]
     bare = {name + "t": entry for name, entry in summed.items()}
     done = run_stage(
         functools.partial(body, count), arrays, outs, scratch, sems, 1, bare.items(), alias.items()

time: 241 us -> 241 us (level)
  no operation moved by 1% of the time
where the time goes in v2:
time: 241 us; the launch traced here: 237 us
  Pallas kernels  236 us (98%)
    pallas_call x2, Pallas kernels, run_stage(): pl.pallas_call(kernel, out_shape=tuple((jax.ShapeDtypeStruct(shape, kind)...  236 us

profile of v2, /device:TPU:0, one launch (start us, length us, event | category | flops | bytes accessed | tf_op | source)
XLA Modules:
  0.0 237.3 jit_solution(9915010461737714881)
XLA Ops:
  0.7 228.4 %shard_map.373 = (bf16[256,1024]{1,0:T(8,128)(2,1)}, bf16[256,1024]{1,0:T(8,128)(2,1)}, bf16[640,1024]{1,0:T(8,128)(2,1)}, bf16[1024,640]{1,0:T(8,128)(2,1)}, bf...) custom-call(bf16[256,1024]{1,0:T(8,128)(2,1)} %refs_0_.1, ...), custom_call_target="tpu_custom_call" | custom-call | tf_op jit(solution)/shard_map/pallas_call | solution.py:140
  229.1 7.9 %shard_map.374 = (f32[16,256]{1,0:T(8,128)}, f32[16,256]{1,0:T(8,128)}, f32[16,256]{1,0:T(8,128)}, f32[16,256]{1,0:T(8,128)}, f32[16,256]{1,0:T(8,128)}, /*index...) custom-call(bf16[256,1024]{1,0:T(8,128)(2,1)} %get-tuple-element.52., ...), custom_call_target="tpu_custom_call" | custom-call | tf_op jit(solution)/shard_map/pallas_call | solution.py:140
